TPU v7x, 512 devices: a whole 4x8x8 slice. The times are simulated.
512 devices in a mesh: row: 16 (over z, core), col: 32 (over x, y).
Axes of the slice: x: 4, y: 8, z: 8, core: 2. Of those that a mesh axis runs over, the one named last changes fastest.
Arguments:
- tensor3: bfloat16 [512, 2048, 512], P('row', 'col'), may hold values from -6 to 6
- pair_mask: int32 [8, 32], P(None, 'col'), may hold values 0 or 1
- g_occ: bfloat16 [512, 512], replicated, may hold values from -0.25 to 0.25
- g_virt_band: bfloat16 [2048, 192], P('col'), may hold values from -0.4375 to 0.4375
Outputs:
- chi: float32 [512, 512], P('row', 'col')
All inputs are finite; a program needn't handle non-finite values. No bound on the sum of `pair_mask` on one device may be relied on, other than what follows from the above.
Results may differ from a plain program's by a relative error of at most 0.0041.
Values may be sent and summed in bfloat16 or wider, within the bound.
A program may use at most 64 MiB of HBM per device.

v0:
```python
import math

import jax
import jax.numpy as jnp
from jax import lax
from jax.sharding import PartitionSpec as P


def extended_2(block, sides, width):
    for axis, dim in sides:
        count = lax.axis_size(axis)
        forward = [(i, i + 1) for i in range(count - 1)]
        backward = [(target, source) for source, target in forward]
        low = lax.ppermute(
            lax.slice_in_dim(block, block.shape[dim] - width, None, axis=dim), axis, forward
        )
        high = lax.ppermute(lax.slice_in_dim(block, 0, width, axis=dim), axis, backward)
        block = jnp.concatenate([low, block, high], axis=dim)
    return block


def on_device(tensor3, pair_mask, g_occ, g_virt_band):
    aux_rows, local_cols, orbitals = tensor3.shape
    block = g_virt_band.shape[1] // 3
    blocks_here = local_cols // block
    mu_blocks = orbitals // block
    groups = lax.axis_size("row")
    share = orbitals // groups
    keep = jnp.transpose(pair_mask).astype(jnp.bfloat16)
    shaped = tensor3.reshape(aux_rows, blocks_here, block, mu_blocks, block)
    masked = (shaped * keep[None, :, None, :, None]).reshape(aux_rows, local_cols, orbitals)
    occ_split = g_occ.reshape(orbitals, groups, share)
    occ_part = jnp.einsum("plm,mrc->prlc", masked, occ_split, preferred_element_type=jnp.float32)
    occ_part = occ_part.astype(jnp.bfloat16).reshape(aux_rows, groups, local_cols * share)
    extended = extended_2(masked, (("col", 1),), block)
    window = extended.reshape(aux_rows, 3 * block, groups, share)
    pieces = jnp.einsum("qsrc,ls->qrlc", window, g_virt_band, preferred_element_type=jnp.float32)
    joined = pieces.astype(jnp.bfloat16)
    virt_part = joined.reshape(aux_rows, groups, local_cols * share)
    occ_moved, virt_moved = (
        lax.all_to_all(occ_part, "row", split_axis=1, concat_axis=0, tiled=True),
        lax.all_to_all(virt_part, "row", split_axis=1, concat_axis=0, tiled=True),
    )
    total_aux = occ_moved.shape[0]
    occ_flat = occ_moved.reshape(total_aux, local_cols * share)
    virt_flat = virt_moved.reshape(total_aux, local_cols * share)
    partial_chi = lax.dot_general(
        occ_flat, virt_flat, (((1,), (1,)), ((), ())), preferred_element_type=jnp.float32
    )
    factor = 1.0 / math.sqrt(orbitals * local_cols * lax.axis_size("col"))
    by_columns = lax.psum_scatter(partial_chi, "col", scatter_dimension=1, tiled=True)
    summed = lax.psum_scatter(by_columns, "row", scatter_dimension=0, tiled=True)
    return summed * factor


def solution(mesh):
    return jax.shard_map(
        on_device,
        mesh=mesh,
        in_specs=(P("row", "col", None), P(None, "col"), P(), P("col", None)),
        out_specs=P("row", "col"),
        check_vma=False,
    )
```

profile of v0, /device:TPU:10, one launch (start us, length us, event | category | flops | bytes accessed | tf_op | source)
XLA Modules:
  0.0 480.5 jit_solution(2210248271824437173)
XLA Ops:
  6.5 0.0 copy-start
  6.5 0.7 convert_bitcast_fusion.2
  7.2 0.1 mul.21
  7.3 0.1 mul.22
  7.4 1.3 copy.17
  8.6 1.7 broadcast_multiply_fusion
  10.4 3.9 convert_bitcast_fusion.1
  14.3 8.5 %copy.27 = bf16[32,16,64,32]{3,2,0,1:T(8,128)(2,1)} copy(bf16[32,16,64,32]{2,3,1,0:T(8,128)(2,1)} %convert_bitcast_fusion.1) | data formatting | bytes 4194304 | tf_op jit(solution)/shard_map/reshape | solution.py:34
  22.7 12.1 %reshape.46 = bf16[32,16,2048]{2,0,1:T(8,128)(2,1)} reshape(bf16[32,16,64,32]{3,2,0,1:T(8,128)(2,1)} %copy.27) | data formatting | bytes 4194304 | tf_op jit(solution)/shard_map/reshape | solution.py:34
  34.8 10.5 %all-to-all-start = ((bf16[32,16,2048]{2,0,1:T(8,128)(2,1)}), bf16[32,16,2048]{2,0,1:T(8,128)(2,1)}, u32[]{:S(2)}, u32[]{:S(2)}) async-start(bf16[32,16,2048]{2,0,1:T(8,128)(2,1)} %reshape.46), calls=%async_computation | async-start | bytes 4194304 | tf_op jit(solution)/shard_map/all_to_all | solution.py:41
  45.3 0.0 reduce-scatter.5.cloned.1.call-start
  45.3 2.4 collective-permute-start.1
  47.7 3.5 collective-permute-start
  51.2 3.2 copy.21
  54.4 40.8 %collective-permute-done.1 = bf16[32,64,512]{2,1,0:T(8,128)(2,1)} collective-permute-done((bf16[32,64,512]{2,1,0:T(8,128)(2,1)S(1)}, bf16[32,64,512]{2,1,0:T(8,128)(2,1)}, u32[]{:S(2)}, u32[]{:S(2)}) %collective-permute-start.1) | collective-permute-done | bytes 2097184 | tf_op jit(solution)/shard_map/ppermute | solution.py:17
  95.2 4.8 copy.22
  100.0 0.0 collective-permute-done
  100.0 4.8 %copy.20 = bf16[32,64,512]{1,2,0:T(8,128)(2,1)} copy(bf16[32,64,512]{2,1,0:T(8,128)(2,1)} %collective-permute-done) | data formatting | bytes 4194304 | tf_op jit(solution)/shard_map/ppermute | solution.py:14
  104.8 0.0 copy-done
  104.8 8.3 %convert_bitcast_fusion = bf16[32,16,64,32]{2,3,1,0:T(8,128)(2,1)} fusion(bf16[32,64,16,32]{1,3,2,0:T(8,128)(2,1)} %bitcast.45, bf16[32,64,16,32]{1,3,2,0:T(8,128)(2,1)} %bitcast.44, bf16[32,64,16,32]{1,3,2,0:T(8,128)(2,1)} %bitcast.46, bf16[64,192]{1,0:T(8,128)(2,1)S(1)} %copy-done), kind=kOutput, calls=%fused_computation.6 | convolution fusion | flops 422576128 | bytes 8413184 | tf_op jit(solution)/shard_map/qsrc,ls->qrlc/dot_general | solution.py:37
  113.1 8.5 %copy.28 = bf16[32,16,64,32]{3,2,0,1:T(8,128)(2,1)} copy(bf16[32,16,64,32]{2,3,1,0:T(8,128)(2,1)} %convert_bitcast_fusion) | data formatting | bytes 4194304 | tf_op jit(solution)/shard_map/reshape | solution.py:39
  121.6 11.1 %reshape.47 = bf16[32,16,2048]{2,0,1:T(8,128)(2,1)S(1)} reshape(bf16[32,16,64,32]{3,2,0,1:T(8,128)(2,1)} %copy.28) | data formatting | bytes 4194304 | tf_op jit(solution)/shard_map/reshape | solution.py:39
  132.7 0.0 all-to-all-done
  132.7 56.5 %all_to_all.30 = bf16[32,16,2048]{2,0,1:T(8,128)(2,1)S(1)} all-to-all(bf16[32,16,2048]{2,0,1:T(8,128)(2,1)S(1)} %reshape.47), channel_id=1, replica_groups=mesh['row'=16,'col'=32] {'row'}, dimensions={1} | all-to-all | bytes 4194304 | tf_op jit(solution)/shard_map/all_to_all | solution.py:42
  189.2 3.8 fusion.11
  193.1 0.0 reduce-scatter.5.cloned.1.call-update
  193.1 0.0 reduce-scatter.7.cloned.1.call-start
  193.1 216.7 %reduce-scatter.5.cloned.1.call-done = f32[512,16]{0,1:T(8,128)} async-done(((f32[512,512]{0,1:T(8,128)}), f32[512,16]{0,1:T(8,128)}) %reduce-scatter.5.cloned.1.call-update) | async-done | bytes 32784 | tf_op jit(solution)/shard_map/reduce_scatter | solution.py:51
  409.8 1.6 copy.29
  411.4 0.0 reduce-scatter.7.cloned.1.call-update
  411.4 60.8 %reduce-scatter.7.cloned.1.call-done = f32[32,16]{1,0:T(8,128)} async-done(((f32[512,16]{1,0:T(8,128)}), f32[32,16]{1,0:T(8,128)}) %reduce-scatter.7.cloned.1.call-update) | async-done | bytes 2064
  472.2 0.8 copy.30
  473.0 0.6 broadcast_multiply_fusion.1
Async XLA Ops:
  6.5 98.3 %copy-start = (bf16[64,192]{1,0:T(8,128)(2,1)S(1)}, bf16[64,192]{1,0:T(8,128)(2,1)}, u32[]{:S(2)}) copy-start(bf16[64,192]{1,0:T(8,128)(2,1)} %param.7) | copy-start | bytes 73732
  34.8 97.9 %all-to-all-start = ((bf16[32,16,2048]{2,0,1:T(8,128)(2,1)}), bf16[32,16,2048]{2,0,1:T(8,128)(2,1)}, u32[]{:S(2)}, u32[]{:S(2)}) async-start(bf16[32,16,2048]{2,0,1:T(8,128)(2,1)} %reshape.46), calls=%async_computation | async-start | bytes 4194304 | tf_op jit(solution)/shard_map/all_to_all | solution.py:41
  45.3 364.5 %reduce-scatter.5.cloned.1.call-start = ((), (), s32[]{:S(2)}) async-start(), calls=%async_computation.4 | async-start | bytes 1081344 | tf_op jit(solution)/shard_map/reduce_scatter | solution.py:51
  45.3 49.9 %collective-permute-start.1 = (bf16[32,64,512]{2,1,0:T(8,128)(2,1)S(1)}, bf16[32,64,512]{2,1,0:T(8,128)(2,1)}, u32[]{:S(2)}, u32[]{:S(2)}) collective-permute-start(bf16[32,64,512]{2,1,0:T(8,128)(2,1)S(1)} %broadcast_multiply_fusion), channel_id=1, source_target_pairs={{1,0},{2,1},{3,2},{4,3},{5,4},{6,5},{7,6},{8,7},{9,8},{10,9},{11,1... | collective-permute-start | bytes 6291464 | tf_op jit(solution)/shard_map/ppermute | solution.py:17
  47.7 52.3 %collective-permute-start = (bf16[32,64,512]{2,1,0:T(8,128)(2,1)S(1)}, bf16[32,64,512]{2,1,0:T(8,128)(2,1)}, u32[]{:S(2)}, u32[]{:S(2)}) collective-permute-start(bf16[32,64,512]{2,1,0:T(8,128)(2,1)S(1)} %broadcast_multiply_fusion), channel_id=1, source_target_pairs={{0,1},{1,2},{2,3},{3,4},{4,5},{5,6},{6,7},{7,8},{8,9},{9,10},{10,1... | collective-permute-start | bytes 6291464 | tf_op jit(solution)/shard_map/ppermute | solution.py:14
  193.1 279.2 %reduce-scatter.7.cloned.1.call-start = ((), (), s32[]{:S(2)}) async-start(), calls=%async_computation.5 | async-start | bytes 278528
Sparse Core Ops, SparseCore 0:
  193.2 216.5 reduce-scatter.4
  412.6 59.6 reduce-scatter.6
where the time goes:
time: 482 us; the launch traced here: 480 us
  waiting for transfers between devices  318 us (66%)
  local copies, waits for them, and re-layouts  56.7 us (12%)
  blocking collectives  56.5 us (12%)
  starting transfers between devices  16.4 us (3%)
  matrix products  16 us (3%)
  between operations  13.5 us (3%)
    reduce_scatter x1, waiting for transfers between devices, on_device(): lax.psum_scatter(partial_chi, 'col', scatter_dimension=1, tiled=True)  217 us
    unnamed x3, waiting for transfers between devices  60.9 us
    all_to_all x1, blocking collectives, on_device(): lax.all_to_all(virt_part, 'row', split_axis=1, concat_axis=0, tiled=True)  56.5 us
    ppermute x1, waiting for transfers between devices, extended_2(): lax.ppermute(lax.slice_in_dim(block, 0, width, axis=dim), axis, backward)  40.8 us
    reshape x2, local copies, waits for them, and re-layouts, on_device(): occ_part.astype(jnp.bfloat16).reshape(aux_rows, groups, local_cols * share)  20.6 us
    reshape x2, local copies, waits for them, and re-layouts, on_device(): virt_part = joined.reshape(aux_rows, groups, local_cols * share)  19.6 us
    all_to_all x1, starting transfers between devices, on_device(): lax.all_to_all(occ_part, 'row', split_axis=1, concat_axis=0, tiled=True)  10.5 us
  transfers between devices with their start and end apart: 5, of which 3 were waited for; matrix products, arithmetic and copies ran while one was open for 8% of the time, Pallas kernels for 0%

commit v1 on v0

v1 whole, which is shorter than its diff:
```python
import math

import jax
import jax.numpy as jnp
from jax import lax
from jax.experimental import pallas as pl
from jax.experimental.pallas import tpu as pltpu
from jax.sharding import PartitionSpec as P

MESH = pl.DeviceIdType.MESH
ROWS, NX, NY = 16, 4, 8
COLS = NX * NY
BS, AUX, ORB = 64, 32, 512
LANES, PIECE = 128, 16
F32, BF16 = jnp.float32, jnp.bfloat16


def remote(src, dst, send, recv, where):
    return pltpu.make_async_remote_copy(
        src_ref=src, dst_ref=dst, send_sem=send, recv_sem=recv, device_id=where, device_id_type=MESH
    )


def kernel(
    m_ref, pm_ref, g_ref, gv_ref, out_ref,
    mk, halo, a_send, b_send, a_in, b_in, acc, xs, xr, ys, yr, zs, zr, tr,
    h_ss, h_rs, a_ss, a_rs, b_ss, b_rs, x_ss, x_rs, y_ss, y_rs, z_ss, z_rs,
):
    r = lax.axis_index("row")
    c = lax.axis_index("col")
    x, y = c // NY, c % NY
    lg_me, ng_me = r // 4, r % 4

    barrier = pltpu.get_barrier_semaphore()

    def greet(where):
        pl.semaphore_signal(barrier, inc=1, device_id=where, device_id_type=MESH)

    @pl.loop(1, ROWS)
    def _(k):
        greet({"row": (r + k) % ROWS})

    for k in range(1, NX):
        greet({"col": ((x + k) % NX) * NY + y})

    @pl.loop(1, NY)
    def _(k):
        greet({"col": x * NY + (y + k) % NY})

    @pl.when(c > 0)
    def _():
        greet({"col": c - 1})

    @pl.when(c < COLS - 1)
    def _():
        greet({"col": c + 1})

    kept = (pm_ref[...] > 0).astype(F32)
    lane = lax.broadcasted_iota(jnp.int32, (8, ORB), 1) // BS
    rows8 = lax.broadcasted_iota(jnp.int32, (8, ORB), 0)
    keep = jnp.sum(jnp.where(lane == rows8, jnp.broadcast_to(kept, (8, ORB)), 0.0), axis=0, keepdims=True)

    both = (c > 0).astype(jnp.int32) + (c < COLS - 1).astype(jnp.int32)
    pl.semaphore_wait(barrier, ROWS - 1 + NX - 1 + NY - 1 + both)

    def to_right(ng):
        return remote(mk.at[ng], halo.at[0, ng], h_ss.at[0, ng], h_rs.at[0, ng], {"col": c + 1})

    def to_left(ng):
        return remote(mk.at[ng], halo.at[1, ng], h_ss.at[1, ng], h_rs.at[1, ng], {"col": c - 1})

    for ng in range(4):
        k_ng = keep[:, ng * LANES:(ng + 1) * LANES].astype(BF16).reshape(1, LANES)

        @pl.loop(0, AUX)
        def _(p):
            mk[ng, p] = m_ref[p, :, ng * LANES:(ng + 1) * LANES] * k_ng

        @pl.when(c < COLS - 1)
        def _():
            to_right(ng).start()

        @pl.when(c > 0)
        def _():
            to_left(ng).start()

    @pl.when(c == 0)
    def _():
        halo[0] = jnp.zeros((4, AUX, BS, LANES), BF16)

    @pl.when(c == COLS - 1)
    def _():
        halo[1] = jnp.zeros((4, AUX, BS, LANES), BF16)

    @pl.loop(0, 4)
    def _(lg):
        for ph in range(2):
            rows = [
                mk[ng, ph * 16:(ph + 1) * 16, pl.ds(pl.multiple_of(lg * 16, 16), 16), :].reshape(256, LANES)
                for ng in range(4)
            ]
            left = jnp.concatenate(rows, axis=1)
            for nh in range(2):
                part = jnp.dot(left, g_ref[:, nh * 256:(nh + 1) * 256], preferred_element_type=F32)
                for ns in range(2):
                    piece = part[:, ns * LANES:(ns + 1) * LANES].reshape(16, 16, LANES)
                    piece = jnp.transpose(piece, (1, 0, 2)).astype(BF16)
                    a_send[nh * 2 + ns, pl.ds(lg * 16, 16), ph * 16:(ph + 1) * 16, :] = piece

    def send_a(d):
        return remote(
            a_send.at[d % 4, pl.ds((d // 4) * 16, 16)], a_in.at[r], a_ss.at[d], a_rs.at[r], {"row": d}
        )

    def send_b(d):
        return remote(
            b_send.at[d % 4, pl.ds((d // 4) * 16, 16)], b_in.at[r], b_ss.at[d], b_rs.at[r], {"row": d}
        )

    @pl.loop(0, ROWS - 1)
    def _(i):
        half = i // 2 + 1
        step = half + (i % 2) * (ROWS - 2 * half)
        send_a((r + step) % ROWS).start()

    a_in[r] = a_send[ng_me, pl.ds(lg_me * 16, 16)]

    band = gv_ref[...]
    for ng in range(4):
        @pl.when(c > 0)
        def _():
            to_right(ng).wait_recv()

        @pl.when(c < COLS - 1)
        def _():
            to_left(ng).wait_recv()

        @pl.loop(0, 2)
        def _(qh):
            outs = []
            for qp in range(8):
                wide = []
                for q in range(2):
                    at = qh * 16 + qp * 2 + q
                    wide.append(jnp.concatenate([halo[0, ng, at], mk[ng, at], halo[1, ng, at]], axis=0))
                prod = jnp.dot(band, jnp.concatenate(wide, axis=1), preferred_element_type=F32)
                outs += [prod[:, :LANES], prod[:, LANES:]]
            full = jnp.transpose(jnp.stack(outs, axis=0), (1, 0, 2)).astype(BF16)
            b_send[ng, :, pl.ds(pl.multiple_of(qh * 16, 16), 16), :] = full

        @pl.loop(0, 4)
        def _(j):
            d = ((lg_me + j) % 4) * 4 + ng

            @pl.when(d != r)
            def _():
                send_b(d).start()

    b_in[r] = b_send[ng_me, pl.ds(lg_me * 16, 16)]

    @pl.loop(1, ROWS)
    def _(k):
        s = (r + k) % ROWS
        remote(a_send.at[0, pl.ds(0, 16)], a_in.at[s], a_ss.at[s], a_rs.at[s], {"row": s}).wait_recv()

    acc[...] = jnp.zeros_like(acc)

    @pl.loop(1, ROWS)
    def _(k):
        s = (r + k) % ROWS
        remote(b_send.at[0, pl.ds(0, 16)], b_in.at[s], b_ss.at[s], b_rs.at[s], {"row": s}).wait_recv()

    @pl.loop(0, 8)
    def _(l):
        def pair(ref):
            return jnp.concatenate(
                [ref[:, 2 * l].reshape(512, LANES), ref[:, 2 * l + 1].reshape(512, LANES)], axis=1
            )
        acc[...] += lax.dot_general(
            pair(b_in), pair(a_in), (((1,), (1,)), ((), ())), preferred_element_type=F32
        )

    for i in range(NX):
        xs[i] = acc[i * 128:(i + 1) * 128, :].astype(BF16)

    def send_x(k):
        to = (x + k) % NX
        return remote(xs.at[to], xr.at[k], x_ss.at[k], x_rs.at[k], {"col": to * NY + y})

    for k in range(1, NX):
        send_x(k).start()
    for k in range(1, NX):
        send_x(k).wait_recv()
    mine = acc[pl.ds(pl.multiple_of(x * 128, 128), 128), :]
    for k in range(1, NX):
        mine = mine + xr[k].astype(F32)

    for i in range(NY):
        ys[i] = mine[i * 16:(i + 1) * 16, :].astype(BF16)
    acc[0:128, :] = mine

    def send_y(k):
        to = (y + k) % NY
        return remote(ys.at[to], yr.at[k], y_ss.at[k], y_rs.at[k], {"col": x * NY + to})

    for k in range(1, NY):
        send_y(k).start()
    for k in range(1, NY):
        send_y(k).wait_recv()
    own = acc[pl.ds(pl.multiple_of(y * 16, 16), 16), :]
    for k in range(1, NY):
        own = own + yr[k].astype(F32)
    for i in range(4):
        zs[i] = own[:, i * LANES:(i + 1) * LANES]

    def send_z(k):
        to = (r + k) % ROWS
        return remote(zs.at[to // 4], zr.at[k], z_ss.at[k], z_rs.at[k], {"row": to})

    @pl.loop(1, ROWS)
    def _(k):
        send_z(k).start()

    zr[0] = zs[lg_me]

    @pl.loop(1, ROWS)
    def _(k):
        send_z(k).wait_recv()

    total = jnp.sum(zr[...], axis=0)
    tr[...] = jnp.transpose(total, (1, 0))
    factor = 1.0 / math.sqrt(ORB * BS * COLS)
    out_ref[...] = tr[pl.ds(pl.multiple_of(ng_me * AUX, AUX), AUX), :] * factor

    for ng in range(4):
        @pl.when(c < COLS - 1)
        def _():
            to_right(ng).wait_send()

        @pl.when(c > 0)
        def _():
            to_left(ng).wait_send()

    @pl.loop(1, ROWS)
    def _(k):
        d = (r + k) % ROWS
        send_a(d).wait_send()
        send_b(d).wait_send()
        send_z(k).wait_send()

    for k in range(1, NX):
        send_x(k).wait_send()
    for k in range(1, NY):
        send_y(k).wait_send()


def on_device(tensor3, pair_mask, g_occ, g_virt_band):
    vmem = pl.BlockSpec(memory_space=pltpu.VMEM)
    dma = pltpu.SemaphoreType.DMA
    return pl.pallas_call(
        kernel,
        out_shape=jax.ShapeDtypeStruct((AUX, 16), F32),
        in_specs=[vmem] * 4,
        out_specs=vmem,
        scratch_shapes=[
            pltpu.VMEM((4, AUX, BS, LANES), BF16),
            pltpu.VMEM((2, 4, AUX, BS, LANES), BF16),
            pltpu.VMEM((4, BS, AUX, LANES), BF16),
            pltpu.VMEM((4, BS, AUX, LANES), BF16),
            pltpu.VMEM((ROWS, PIECE, AUX, LANES), BF16),
            pltpu.VMEM((ROWS, PIECE, AUX, LANES), BF16),
            pltpu.VMEM((512, 512), F32),
            pltpu.VMEM((NX, 128, 512), BF16),
            pltpu.VMEM((NX, 128, 512), BF16),
            pltpu.VMEM((NY, 16, 512), BF16),
            pltpu.VMEM((NY, 16, 512), BF16),
            pltpu.VMEM((4, 16, LANES), F32),
            pltpu.VMEM((ROWS, 16, LANES), F32),
            pltpu.VMEM((LANES, 16), F32),
            dma((2, 4)), dma((2, 4)),
            dma((ROWS,)), dma((ROWS,)), dma((ROWS,)), dma((ROWS,)),
            dma((NX,)), dma((NX,)), dma((NY,)), dma((NY,)), dma((ROWS,)), dma((ROWS,)),
        ],
        compiler_params=pltpu.CompilerParams(
            collective_id=0, has_side_effects=True, vmem_limit_bytes=48 * 1024 * 1024
        ),
        cost_estimate=pl.CostEstimate(flops=2600000000, bytes_accessed=3 << 20, transcendentals=0),
    )(tensor3, pair_mask, g_occ, g_virt_band)


def solution(mesh):
    return jax.shard_map(
        on_device,
        mesh=mesh,
        in_specs=(P("row", "col", None), P(None, "col"), P(), P("col", None)),
        out_specs=P("row", "col"),
        check_vma=False,
    )
```

time: 482 us -> 138 us (0.29)
  the two profiles are of different devices: /device:TPU:10 before, /device:TPU:1 now
where the time goes in v1:
time: 138 us
  Pallas kernels  133 us (96%)
  local copies, waits for them, and re-layouts  4.79 us (3%)
    pallas_call x1, Pallas kernels, on_device(): pl.pallas_call(kernel, out_shape=jax.ShapeDtypeStruct((AUX, 16), F32), in...  133 us
    unnamed x7, local copies, waits for them, and re-layouts  4.12 us

profile of v1, /device:TPU:1, one launch (start us, length us, event | category | flops | bytes accessed | tf_op | source)
XLA Modules:
  0.0 137.8 jit_solution(17553028403767336617)
XLA Ops:
  0.0 0.7 copy.5.pm_ref
  0.7 0.0 copy-start
  0.7 1.6 %copy-done = bf16[32,64,512]{2,1,0:T(8,128)(2,1)S(1)} copy-done((bf16[32,64,512]{2,1,0:T(8,128)(2,1)S(1)}, bf16[32,64,512]{2,1,0:T(8,128)(2,1)}, u32[]{:S(2)}) %copy-start) | copy-done | bytes 2097176
  2.3 0.0 copy-start.1
  2.3 1.0 copy-done.1
  3.4 0.0 copy-start.2
  3.4 0.8 copy-done.2
  4.1 133.0 %shard_map.46 = f32[32,16]{1,0:T(8,128)S(1)} custom-call(bf16[32,64,512]{2,1,0:T(8,128)(2,1)S(1)} %copy-done, s32[8,1]{1,0:T(8,128)S(1)} %copy.5.pm_ref, bf16[512,512]{1,0:T(8,128)(2,1)S(1)} %copy-done.1, bf16[64,192]{1,0:T(8,128)(2,1)S(1)} %copy-done.2), custom_call_target="tpu_custom_call" | custom-call | flops 2600000000 | bytes 3145728 | tf_op jit(solution)/shard_map/pallas_call | solution.py:260
  137.2 0.7 copy.6
Async XLA Ops:
  0.7 1.6 %copy-start = (bf16[32,64,512]{2,1,0:T(8,128)(2,1)S(1)}, bf16[32,64,512]{2,1,0:T(8,128)(2,1)}, u32[]{:S(2)}) copy-start(bf16[32,64,512]{2,1,0:T(8,128)(2,1)} %m_ref.1) | copy-start | bytes 6291460
  2.3 1.0 copy-start.1
  3.4 0.8 copy-start.2

commit v2 on v1

v2 whole, which is shorter than its diff:
```python
import math

import jax
import jax.numpy as jnp
from jax import lax
from jax.experimental import pallas as pl
from jax.experimental.pallas import tpu as pltpu
from jax.sharding import PartitionSpec as P

MESH = pl.DeviceIdType.MESH
ROWS, NX, NY = 16, 4, 8
COLS = NX * NY
BS, AUX, ORB = 64, 32, 512
LANES, PIECE, HALF = 128, 16, 16
F32, BF16 = jnp.float32, jnp.bfloat16


def remote(src, dst, send, recv, where):
    return pltpu.make_async_remote_copy(
        src_ref=src, dst_ref=dst, send_sem=send, recv_sem=recv, device_id=where, device_id_type=MESH
    )


def kernel(
    m_hbm, pm_hbm, g_hbm, gv_hbm, out_ref,
    m_ref, pm_ref, g_ref, gv_ref, mk, halo, a_send, b_send, a_in, b_in,
    acc, part, xs, xr, ys, yr, zs, zr, tr,
    in_s, h_ss, h_rs, a_ss, a_rs, b_ss, b_rs, x_ss, x_rs, y_ss, y_rs, z_ss, z_rs,
):
    r = lax.axis_index("row")
    c = lax.axis_index("col")
    x, y = c // NY, c % NY
    lg_me, ng_me = r // 4, r % 4

    def load_m(i):
        return pltpu.make_async_copy(m_hbm.at[pl.ds(8 * i, 8)], m_ref.at[pl.ds(8 * i, 8)], in_s.at[i])

    load_pm = pltpu.make_async_copy(pm_hbm, pm_ref, in_s.at[4])
    load_g = pltpu.make_async_copy(g_hbm, g_ref, in_s.at[5])
    load_gv = pltpu.make_async_copy(gv_hbm, gv_ref, in_s.at[6])
    load_pm.start()
    for i in range(4):
        load_m(i).start()
    load_g.start()
    load_gv.start()

    barrier = pltpu.get_barrier_semaphore()

    def greet(where):
        pl.semaphore_signal(barrier, inc=1, device_id=where, device_id_type=MESH)

    @pl.loop(1, ROWS)
    def _(k):
        greet({"row": (r + k) % ROWS})

    for k in range(1, NX):
        greet({"col": ((x + k) % NX) * NY + y})

    @pl.loop(1, NY)
    def _(k):
        greet({"col": x * NY + (y + k) % NY})

    @pl.when(c > 0)
    def _():
        greet({"col": c - 1})

    @pl.when(c < COLS - 1)
    def _():
        greet({"col": c + 1})

    load_pm.wait()
    lane = lax.broadcasted_iota(jnp.int32, (1, ORB), 1) // BS
    keep = jnp.zeros((1, ORB), F32)
    for b in range(8):
        kept = jnp.broadcast_to((pm_ref[0:1, b:b + 1] > 0).astype(F32), (1, ORB))
        keep = jnp.where(lane == b, kept, keep)
    keep = keep.astype(BF16)

    for i in range(4):
        load_m(i).wait()

        @pl.loop(8 * i, 8 * i + 8)
        def _(p):
            row = m_ref[p] * keep
            for ng in range(4):
                mk[ng, p] = row[:, ng * LANES:(ng + 1) * LANES]

    def occ(lg):
        for ph in range(2):
            rows = [
                mk[ng, ph * 16:(ph + 1) * 16, pl.ds(pl.multiple_of(lg * 16, 16), 16), :].reshape(256, LANES)
                for ng in range(4)
            ]
            left = jnp.concatenate(rows, axis=1)
            for nh in range(2):
                part = jnp.dot(left, g_ref[:, nh * 256:(nh + 1) * 256], preferred_element_type=F32)
                for ns in range(2):
                    piece = part[:, ns * LANES:(ns + 1) * LANES].reshape(16, 16, LANES)
                    piece = jnp.transpose(piece, (1, 0, 2)).astype(BF16)
                    a_send[nh * 2 + ns, pl.ds(lg * 16, 16), ph * 16:(ph + 1) * 16, :] = piece

    def send_a(d):
        return remote(
            a_send.at[d % 4, pl.ds((d // 4) * 16, 16)], a_in.at[r], a_ss.at[d], a_rs.at[r], {"row": d}
        )

    load_g.wait()

    @pl.loop(0, 4)
    def _(lg):
        occ(lg)

    both = (c > 0).astype(jnp.int32) + (c < COLS - 1).astype(jnp.int32)
    pl.semaphore_wait(barrier, ROWS - 1 + NX - 1 + NY - 1 + both)

    def half_of(ref, g):
        return ref.at[:, pl.ds(HALF * g, HALF)]

    def to_right(g):
        return remote(half_of(mk, g), half_of(halo.at[0], g), h_ss.at[0, g], h_rs.at[0, g], {"col": c + 1})

    def to_left(g):
        return remote(half_of(mk, g), half_of(halo.at[1], g), h_ss.at[1, g], h_rs.at[1, g], {"col": c - 1})

    def ordered(i):
        near = i // 2 + 1
        return (r + near + (i % 2) * (ROWS - 2 * near)) % ROWS

    @pl.loop(0, 4)
    def _(i):
        send_a(ordered(i)).start()

    for g in range(2):
        @pl.when(c < COLS - 1)
        def _():
            to_right(g).start()

        @pl.when(c > 0)
        def _():
            to_left(g).start()

    @pl.loop(4, ROWS - 1)
    def _(i):
        send_a(ordered(i)).start()

    a_in[r] = a_send[ng_me, pl.ds(lg_me * 16, 16)]

    @pl.when(c == 0)
    def _():
        halo[0] = jnp.zeros((4, AUX, BS, LANES), BF16)

    @pl.when(c == COLS - 1)
    def _():
        halo[1] = jnp.zeros((4, AUX, BS, LANES), BF16)

    load_gv.wait()

    def send_b(g, d):
        return remote(
            b_send.at[g, d % 4, pl.ds((d // 4) * 16, 16)], b_in.at[g, r], b_ss.at[g, d], b_rs.at[g, r],
            {"row": d},
        )

    for g in range(2):
        @pl.when(c > 0)
        def _():
            to_right(g).wait_recv()

        @pl.when(c < COLS - 1)
        def _():
            to_left(g).wait_recv()

        @pl.loop(0, 4)
        def _(ng):
            outs = []
            for qp in range(8):
                wide = []
                for q in range(2):
                    at = g * HALF + qp * 2 + q
                    wide.append(jnp.concatenate([halo[0, ng, at], mk[ng, at], halo[1, ng, at]], axis=0))
                prod = jnp.dot(gv_ref[...], jnp.concatenate(wide, axis=1), preferred_element_type=F32)
                outs += [prod[:, :LANES], prod[:, LANES:]]
            b_send[g, ng] = jnp.transpose(jnp.stack(outs, axis=0), (1, 0, 2)).astype(BF16)

        @pl.loop(0, ROWS - 1)
        def _(i):
            send_b(g, ordered(i)).start()

        b_in[g, r] = b_send[g, ng_me, pl.ds(lg_me * 16, 16)]

    @pl.loop(1, ROWS)
    def _(k):
        s = (r + k) % ROWS
        remote(a_send.at[0, pl.ds(0, 16)], a_in.at[s], a_ss.at[s], a_rs.at[s], {"row": s}).wait_recv()

    def send_x(g, k):
        to = (x + k) % NX
        return remote(xs.at[g, k], xr.at[g, k], x_ss.at[g, k], x_rs.at[g, k], {"col": to * NY + y})

    def send_y(g, k):
        to = (y + k) % NY
        return remote(ys.at[g, to // 2], yr.at[k], y_ss.at[g, k], y_rs.at[k], {"col": x * NY + to})

    def send_z(k):
        to = (r + k) % ROWS
        return remote(zs.at[to // 4], zr.at[k], z_ss.at[k], z_rs.at[k], {"row": to})

    def chi_rows(g, ahead):
        blocks = [(x + k) % NX for k in ahead]
        for block in blocks:
            @pl.loop(4 * block, 4 * block + 4)
            def _(s):
                @pl.when(s != r)
                def _():
                    remote(
                        b_send.at[g, 0, pl.ds(0, 16)], b_in.at[g, s], b_ss.at[g, s], b_rs.at[g, s], {"row": s}
                    ).wait_recv()

        acc[...] = jnp.zeros_like(acc)

        @pl.loop(0, 8)
        def _(l):
            def pair(at, rows):
                return jnp.concatenate([at(2 * l).reshape(rows, LANES), at(2 * l + 1).reshape(rows, LANES)], axis=1)

            left = jnp.concatenate(
                [pair(lambda n: b_in[g, pl.ds(4 * block, 4), n], 4 * HALF) for block in blocks], axis=0
            )
            acc[...] += lax.dot_general(
                left, pair(lambda n: a_in[:, n], ROWS * AUX), (((1,), (1,)), ((), ())), preferred_element_type=F32
            )

    def sum_y():
        @pl.loop(1, NY)
        def _(k):
            send_y(0, k).wait_recv()

        own = part[pl.ds(pl.multiple_of((y // 2) * 16, 16), 16), :]
        for k in range(1, NY):
            own = own + yr[k].astype(F32)
        for i in range(4):
            zs[i] = own[:, i * LANES:(i + 1) * LANES]

        @pl.loop(1, ROWS)
        def _(k):
            send_z(k).start()

        zr[0] = zs[lg_me]

    for g in range(2):
        chi_rows(g, (2, 1))
        xs[g, 2] = acc[0:64, :].astype(BF16)
        send_x(g, 2).start()
        xs[g, 1] = acc[64:128, :].astype(BF16)
        send_x(g, 1).start()
        chi_rows(g, (3, 0))
        xs[g, 3] = acc[0:64, :].astype(BF16)
        send_x(g, 3).start()
        mine = acc[64:128, :]
        for k in (1, 2, 3):
            send_x(g, k).wait_recv()
            mine = mine + xr[g, k].astype(F32)

        for i in range(4):
            ys[g, i] = mine[i * 16:(i + 1) * 16, :].astype(BF16)

        @pl.loop(1, NY)
        def _(k):
            @pl.when((y + k) % 2 == g)
            def _():
                send_y(g, k).start()

        @pl.when(y % 2 == g)
        def _():
            part[...] = mine
            sum_y()

    @pl.loop(1, ROWS)
    def _(k):
        send_z(k).wait_recv()

    factor = 1.0 / math.sqrt(ORB * BS * COLS)
    tr[...] = jnp.transpose(jnp.sum(zr[...], axis=0), (1, 0))
    out_ref[...] = tr[pl.ds(pl.multiple_of(ng_me * AUX, AUX), AUX), :] * factor

    for g in range(2):
        @pl.when(c < COLS - 1)
        def _():
            to_right(g).wait_send()

        @pl.when(c > 0)
        def _():
            to_left(g).wait_send()

        for k in range(1, NX):
            send_x(g, k).wait_send()

        @pl.loop(1, NY)
        def _(k):
            @pl.when((y + k) % 2 == g)
            def _():
                send_y(g, k).wait_send()

    @pl.loop(1, ROWS)
    def _(k):
        d = (r + k) % ROWS
        send_a(d).wait_send()
        send_b(0, d).wait_send()
        send_b(1, d).wait_send()
        send_z(k).wait_send()


def on_device(tensor3, pair_mask, g_occ, g_virt_band):
    dma = pltpu.SemaphoreType.DMA
    return pl.pallas_call(
        kernel,
        out_shape=jax.ShapeDtypeStruct((AUX, 16), F32),
        in_specs=[pl.BlockSpec(memory_space=pl.ANY)] * 4,
        out_specs=pl.BlockSpec(memory_space=pltpu.VMEM),
        scratch_shapes=[
            pltpu.VMEM((AUX, BS, ORB), BF16),
            pltpu.VMEM((1, 8), jnp.int32),
            pltpu.VMEM((ORB, ORB), BF16),
            pltpu.VMEM((BS, 3 * BS), BF16),
            pltpu.VMEM((4, AUX, BS, LANES), BF16),
            pltpu.VMEM((2, 4, AUX, BS, LANES), BF16),
            pltpu.VMEM((4, BS, AUX, LANES), BF16),
            pltpu.VMEM((2, 4, BS, HALF, LANES), BF16),
            pltpu.VMEM((ROWS, PIECE, AUX, LANES), BF16),
            pltpu.VMEM((2, ROWS, PIECE, HALF, LANES), BF16),
            pltpu.VMEM((128, 512), F32),
            pltpu.VMEM((64, 512), F32),
            pltpu.VMEM((2, NX, 64, 512), BF16),
            pltpu.VMEM((2, NX, 64, 512), BF16),
            pltpu.VMEM((2, 4, 16, 512), BF16),
            pltpu.VMEM((NY, 16, 512), BF16),
            pltpu.VMEM((4, 16, LANES), F32),
            pltpu.VMEM((ROWS, 16, LANES), F32),
            pltpu.VMEM((LANES, 16), F32),
            dma((7,)), dma((2, 2)), dma((2, 2)),
            dma((ROWS,)), dma((ROWS,)), dma((2, ROWS)), dma((2, ROWS)),
            dma((2, NX)), dma((2, NX)), dma((2, NY)), dma((NY,)), dma((ROWS,)), dma((ROWS,)),
        ],
        compiler_params=pltpu.CompilerParams(
            collective_id=0, has_side_effects=True, vmem_limit_bytes=60 * 1024 * 1024
        ),
        cost_estimate=pl.CostEstimate(flops=2600000000, bytes_accessed=3 << 20, transcendentals=0),
    )(tensor3, pair_mask.T, g_occ, g_virt_band)


def solution(mesh):
    return jax.shard_map(
        on_device,
        mesh=mesh,
        in_specs=(P("row", "col", None), P(None, "col"), P(), P("col", None)),
        out_specs=P("row", "col"),
        check_vma=False,
    )
```

time: 138 us -> 130 us (0.942)
  the two profiles are of different devices: /device:TPU:1 before, /device:TPU:9 now
where the time goes in v2:
time: 130 us
  Pallas kernels  129 us (99%)
  local copies, waits for them, and re-layouts  1.39 us (1%)
    pallas_call x1, Pallas kernels, on_device(): pl.pallas_call(kernel, out_shape=jax.ShapeDtypeStruct((AUX, 16), F32), in...  129 us

profile of v2, /device:TPU:9, one launch (start us, length us, event | category | flops | bytes accessed | tf_op | source)
XLA Modules:
  0.0 130.0 jit_solution(6343908239465538486)
XLA Ops:
  0.0 128.6 %shard_map.46 = f32[32,16]{1,0:T(8,128)} custom-call(bf16[32,64,512]{2,1,0:T(8,128)(2,1)} %m_hbm.1, s32[1,8]{1,0:T(1,128)} %bitcast.1, bf16[512,512]{1,0:T(8,128)(2,1)} %g_hbm.1, bf16[64,192]{1,0:T(8,128)(2,1)} %gv_hbm.1), custom_call_target="tpu_custom_call" | custom-call | flops 2600000000 | bytes 3145728 | tf_op jit(solution)/shard_map/pallas_call | solution.py:315
  128.6 1.4 %copy.5 = f32[32,16]{0,1:T(8,128)} copy(f32[32,16]{1,0:T(8,128)} %shard_map.46) | data formatting | bytes 4096 | tf_op jit(solution)/shard_map/pallas_call | solution.py:315

commit v3 on v2

--- a/solution.py
+++ b/solution.py
@@ -122,9 +122,12 @@
     def to_left(g):
         return remote(half_of(mk, g), half_of(halo.at[1], g), h_ss.at[1, g], h_rs.at[1, g], {"col": c - 1})
 
+    def steps(i, count):
+        near = (count - 1 - i) // 2 + 1
+        return near + ((count - 1 - i) % 2) * (count + 1 - 2 * near)
+
     def ordered(i):
-        near = i // 2 + 1
-        return (r + near + (i % 2) * (ROWS - 2 * near)) % ROWS
+        return (r + steps(i, ROWS - 1)) % ROWS
 
     @pl.loop(0, 4)
     def _(i):
@@ -203,7 +206,7 @@
 
     def send_z(k):
         to = (r + k) % ROWS
-        return remote(zs.at[to // 4], zr.at[k], z_ss.at[k], z_rs.at[k], {"row": to})
+        return remote(zs.at[to // 4, to % 2], zr.at[k], z_ss.at[k], z_rs.at[k], {"row": to})
 
     def chi_rows(g, ahead):
         blocks = [(x + k) % NX for k in ahead]
@@ -216,18 +219,15 @@
                         b_send.at[g, 0, pl.ds(0, 16)], b_in.at[g, s], b_ss.at[g, s], b_rs.at[g, s], {"row": s}
                     ).wait_recv()
 
-        acc[...] = jnp.zeros_like(acc)
-
-        @pl.loop(0, 8)
-        def _(l):
-            def pair(at, rows):
-                return jnp.concatenate([at(2 * l).reshape(rows, LANES), at(2 * l + 1).reshape(rows, LANES)], axis=1)
-
-            left = jnp.concatenate(
-                [pair(lambda n: b_in[g, pl.ds(4 * block, 4), n], 4 * HALF) for block in blocks], axis=0
-            )
-            acc[...] += lax.dot_general(
-                left, pair(lambda n: a_in[:, n], ROWS * AUX), (((1,), (1,)), ((), ())), preferred_element_type=F32
+        def wide(at, rows):
+            return jnp.concatenate([at(n).reshape(rows, LANES) for n in range(PIECE)], axis=1)
+
+        left = jnp.concatenate(
+            [wide(lambda n: b_in[g, pl.ds(4 * block, 4), n], 4 * HALF) for block in blocks], axis=0
+        )
+        for p in range(2):
+            acc[:, 256 * p:256 * p + 256] = lax.dot_general(
+                left, wide(lambda n: a_in[8 * p:8 * p + 8, n], 256), (((1,), (1,)), ((), ())), preferred_element_type=F32
             )
 
     def sum_y():
@@ -238,14 +238,17 @@
         own = part[pl.ds(pl.multiple_of((y // 2) * 16, 16), 16), :]
         for k in range(1, NY):
             own = own + yr[k].astype(F32)
+        lanes = lax.broadcasted_iota(jnp.int32, (8, LANES), 1) // AUX
         for i in range(4):
-            zs[i] = own[:, i * LANES:(i + 1) * LANES]
-
-        @pl.loop(1, ROWS)
-        def _(k):
-            send_z(k).start()
-
-        zr[0] = zs[lg_me]
+            upper, lower = own[:8, i * LANES:(i + 1) * LANES], own[8:, i * LANES:(i + 1) * LANES]
+            zs[i, 0] = jnp.where(lanes % 2 == 0, upper, pltpu.roll(lower, AUX, 1))
+            zs[i, 1] = jnp.where(lanes % 2 == 1, upper, pltpu.roll(lower, AUX, 1))
+
+        @pl.loop(0, ROWS - 1)
+        def _(i):
+            send_z(steps(i, ROWS - 1)).start()
+
+        zr[0] = zs[lg_me, ng_me % 2]
 
     for g in range(2):
         chi_rows(g, (2, 1))
@@ -264,8 +267,10 @@
         for i in range(4):
             ys[g, i] = mine[i * 16:(i + 1) * 16, :].astype(BF16)
 
-        @pl.loop(1, NY)
-        def _(k):
+        @pl.loop(0, NY - 1)
+        def _(i):
+            k = steps(i, NY - 1)
+
             @pl.when((y + k) % 2 == g)
             def _():
                 send_y(g, k).start()
@@ -281,7 +286,9 @@
 
     factor = 1.0 / math.sqrt(ORB * BS * COLS)
     tr[...] = jnp.transpose(jnp.sum(zr[...], axis=0), (1, 0))
-    out_ref[...] = tr[pl.ds(pl.multiple_of(ng_me * AUX, AUX), AUX), :] * factor
+    upper = tr[pl.ds(pl.multiple_of(ng_me * AUX, AUX), AUX), :]
+    lower = tr[pl.ds(pl.multiple_of((ng_me + 1) % 4 * AUX, AUX), AUX), :]
+    out_ref[...] = jnp.concatenate([upper, lower], axis=1) * factor
 
     for g in range(2):
         @pl.when(c < COLS - 1)
@@ -334,9 +341,9 @@
             pltpu.VMEM((2, NX, 64, 512), BF16),
             pltpu.VMEM((2, 4, 16, 512), BF16),
             pltpu.VMEM((NY, 16, 512), BF16),
-            pltpu.VMEM((4, 16, LANES), F32),
-            pltpu.VMEM((ROWS, 16, LANES), F32),
-            pltpu.VMEM((LANES, 16), F32),
+            pltpu.VMEM((4, 2, 8, LANES), F32),
+            pltpu.VMEM((ROWS, 8, LANES), F32),
+            pltpu.VMEM((LANES, 8), F32),
             dma((7,)), dma((2, 2)), dma((2, 2)),
             dma((ROWS,)), dma((ROWS,)), dma((2, ROWS)), dma((2, ROWS)),
             dma((2, NX)), dma((2, NX)), dma((2, NY)), dma((NY,)), dma((ROWS,)), dma((ROWS,)),

time: 130 us -> 126 us (0.969)
  Pallas kernels: 129 us -> 125 us
    pallas_call x1, Pallas kernels: 129 us -> 125 us  [on_device(): pl.pallas_call(kernel, out_shape=jax.ShapeDtypeStruct((AUX, 16), F32), in...]
where the time goes in v3:
time: 126 us
  Pallas kernels  125 us (99%)
  local copies, waits for them, and re-layouts  1.39 us (1%)
    pallas_call x1, Pallas kernels, on_device(): pl.pallas_call(kernel, out_shape=jax.ShapeDtypeStruct((AUX, 16), F32), in...  125 us

profile of v3, /device:TPU:9, one launch (start us, length us, event | category | flops | bytes accessed | tf_op | source)
XLA Modules:
  0.0 126.1 jit_solution(4112596135033637466)
XLA Ops:
  0.0 124.7 %shard_map.46 = f32[32,16]{1,0:T(8,128)} custom-call(bf16[32,64,512]{2,1,0:T(8,128)(2,1)} %m_hbm.1, s32[1,8]{1,0:T(1,128)} %bitcast.1, bf16[512,512]{1,0:T(8,128)(2,1)} %g_hbm.1, bf16[64,192]{1,0:T(8,128)(2,1)} %gv_hbm.1), custom_call_target="tpu_custom_call" | custom-call | flops 2600000000 | bytes 3145728 | tf_op jit(solution)/shard_map/pallas_call | solution.py:322
  124.7 1.4 %copy.5 = f32[32,16]{0,1:T(8,128)} copy(f32[32,16]{1,0:T(8,128)} %shard_map.46) | data formatting | bytes 4096 | tf_op jit(solution)/shard_map/pallas_call | solution.py:322

commit v4 on v3

--- a/solution.py
+++ b/solution.py
@@ -24,7 +24,7 @@
 def kernel(
     m_hbm, pm_hbm, g_hbm, gv_hbm, out_ref,
     m_ref, pm_ref, g_ref, gv_ref, mk, halo, a_send, b_send, a_in, b_in,
-    acc, part, xs, xr, ys, yr, zs, zr, tr,
+    acc, full, part, xs, xr, ys, yr, zs, zr, tr,
     in_s, h_ss, h_rs, a_ss, a_rs, b_ss, b_rs, x_ss, x_rs, y_ss, y_rs, z_ss, z_rs,
 ):
     r = lax.axis_index("row")
@@ -38,35 +38,42 @@
     load_pm = pltpu.make_async_copy(pm_hbm, pm_ref, in_s.at[4])
     load_g = pltpu.make_async_copy(g_hbm, g_ref, in_s.at[5])
     load_gv = pltpu.make_async_copy(gv_hbm, gv_ref, in_s.at[6])
+    def steps(i, count):
+        near = (count - 1 - i) // 2 + 1
+        return near + ((count - 1 - i) % 2) * (count + 1 - 2 * near)
+
+    barrier = pltpu.get_barrier_semaphore()
+
+    def greet(where):
+        pl.semaphore_signal(barrier, inc=1, device_id=where, device_id_type=MESH)
+
+    for i in range(4):
+        greet({"row": (r + steps(i, ROWS - 1)) % ROWS})
+        greet({"col": x * NY + (y + steps(i, NY - 1)) % NY})
+
+    @pl.loop(4, ROWS - 1)
+    def _(i):
+        greet({"row": (r + steps(i, ROWS - 1)) % ROWS})
+
+    for i in range(4, NY - 1):
+        greet({"col": x * NY + (y + steps(i, NY - 1)) % NY})
+
+    for k in range(1, NX):
+        greet({"col": ((x + k) % NX) * NY + y})
+
+    @pl.when(c > 0)
+    def _():
+        greet({"col": c - 1})
+
+    @pl.when(c < COLS - 1)
+    def _():
+        greet({"col": c + 1})
+
     load_pm.start()
     for i in range(4):
         load_m(i).start()
     load_g.start()
     load_gv.start()
-
-    barrier = pltpu.get_barrier_semaphore()
-
-    def greet(where):
-        pl.semaphore_signal(barrier, inc=1, device_id=where, device_id_type=MESH)
-
-    @pl.loop(1, ROWS)
-    def _(k):
-        greet({"row": (r + k) % ROWS})
-
-    for k in range(1, NX):
-        greet({"col": ((x + k) % NX) * NY + y})
-
-    @pl.loop(1, NY)
-    def _(k):
-        greet({"col": x * NY + (y + k) % NY})
-
-    @pl.when(c > 0)
-    def _():
-        greet({"col": c - 1})
-
-    @pl.when(c < COLS - 1)
-    def _():
-        greet({"col": c + 1})
 
     load_pm.wait()
     lane = lax.broadcasted_iota(jnp.int32, (1, ORB), 1) // BS
@@ -122,10 +129,6 @@
     def to_left(g):
         return remote(half_of(mk, g), half_of(halo.at[1], g), h_ss.at[1, g], h_rs.at[1, g], {"col": c - 1})
 
-    def steps(i, count):
-        near = (count - 1 - i) // 2 + 1
-        return near + ((count - 1 - i) % 2) * (count + 1 - 2 * near)
-
     def ordered(i):
         return (r + steps(i, ROWS - 1)) % ROWS
 
@@ -209,7 +212,7 @@
         return remote(zs.at[to // 4, to % 2], zr.at[k], z_ss.at[k], z_rs.at[k], {"row": to})
 
     def chi_rows(g, ahead):
-        blocks = [(x + k) % NX for k in ahead]
+        blocks = [(lg_me + k) % NX for k in ahead]
         for block in blocks:
             @pl.loop(4 * block, 4 * block + 4)
             def _(s):
@@ -226,7 +229,7 @@
             [wide(lambda n: b_in[g, pl.ds(4 * block, 4), n], 4 * HALF) for block in blocks], axis=0
         )
         for p in range(2):
-            acc[:, 256 * p:256 * p + 256] = lax.dot_general(
+            acc[0:64 * len(ahead), 256 * p:256 * p + 256] = lax.dot_general(
                 left, wide(lambda n: a_in[8 * p:8 * p + 8, n], 256), (((1,), (1,)), ((), ())), preferred_element_type=F32
             )
 
@@ -250,16 +253,54 @@
 
         zr[0] = zs[lg_me, ng_me % 2]
 
+    def left_xy(g):
+        for k in range(1, NX):
+            send_x(g, k).wait_send()
+
+        @pl.loop(1, NY)
+        def _(k):
+            @pl.when((y + k) % 2 == g)
+            def _():
+                send_y(g, k).wait_send()
+
+    def left_row(send):
+        @pl.loop(1, ROWS)
+        def _(k):
+            send((r + k) % ROWS).wait_send()
+
     for g in range(2):
-        chi_rows(g, (2, 1))
-        xs[g, 2] = acc[0:64, :].astype(BF16)
-        send_x(g, 2).start()
-        xs[g, 1] = acc[64:128, :].astype(BF16)
-        send_x(g, 1).start()
-        chi_rows(g, (3, 0))
-        xs[g, 3] = acc[0:64, :].astype(BF16)
-        send_x(g, 3).start()
-        mine = acc[64:128, :]
+        if g == 1:
+            for h in range(2):
+                @pl.when(c < COLS - 1)
+                def _():
+                    to_right(h).wait_send()
+
+                @pl.when(c > 0)
+                def _():
+                    to_left(h).wait_send()
+
+            left_row(send_a)
+            left_row(lambda d: send_b(0, d))
+            left_xy(0)
+
+        for ahead in ((2,), (1, 3), (0,)):
+            chi_rows(g, ahead)
+            for at, k in enumerate(ahead):
+                rows = acc[64 * at:64 * at + 64, :]
+                step = (lg_me + k - x + NX) % NX
+
+                @pl.when(step == 0)
+                def _():
+                    full[...] = rows
+
+                @pl.when(step != 0)
+                def _():
+                    xs[g, step] = rows.astype(BF16)
+                    send_x(g, step).start()
+
+        if g == 1:
+            left_row(lambda d: send_b(1, d))
+        mine = full[...]
         for k in (1, 2, 3):
             send_x(g, k).wait_recv()
             mine = mine + xr[g, k].astype(F32)
@@ -279,6 +320,8 @@
         def _():
             part[...] = mine
             sum_y()
+
+    left_xy(1)
 
     @pl.loop(1, ROWS)
     def _(k):
@@ -290,30 +333,8 @@
     lower = tr[pl.ds(pl.multiple_of((ng_me + 1) % 4 * AUX, AUX), AUX), :]
     out_ref[...] = jnp.concatenate([upper, lower], axis=1) * factor
 
-    for g in range(2):
-        @pl.when(c < COLS - 1)
-        def _():
-            to_right(g).wait_send()
-
-        @pl.when(c > 0)
-        def _():
-            to_left(g).wait_send()
-
-        for k in range(1, NX):
-            send_x(g, k).wait_send()
-
-        @pl.loop(1, NY)
-        def _(k):
-            @pl.when((y + k) % 2 == g)
-            def _():
-                send_y(g, k).wait_send()
-
     @pl.loop(1, ROWS)
     def _(k):
-        d = (r + k) % ROWS
-        send_a(d).wait_send()
-        send_b(0, d).wait_send()
-        send_b(1, d).wait_send()
         send_z(k).wait_send()
 
 
@@ -337,6 +358,7 @@
             pltpu.VMEM((2, ROWS, PIECE, HALF, LANES), BF16),
             pltpu.VMEM((128, 512), F32),
             pltpu.VMEM((64, 512), F32),
+            pltpu.VMEM((64, 512), F32),
             pltpu.VMEM((2, NX, 64, 512), BF16),
             pltpu.VMEM((2, NX, 64, 512), BF16),
             pltpu.VMEM((2, 4, 16, 512), BF16),

time: 126 us -> 126 us (level)
  no operation moved by 1% of the time
where the time goes in v4:
time: 126 us
  Pallas kernels  124 us (98%)
  local copies, waits for them, and re-layouts  1.39 us (1%)
    pallas_call x1, Pallas kernels, on_device(): pl.pallas_call(kernel, out_shape=jax.ShapeDtypeStruct((AUX, 16), F32), in...  124 us

profile of v4, /device:TPU:9, one launch (start us, length us, event | category | flops | bytes accessed | tf_op | source)
XLA Modules:
  0.0 125.5 jit_solution(7491243471561577868)
XLA Ops:
  0.0 124.1 %shard_map.46 = f32[32,16]{1,0:T(8,128)} custom-call(bf16[32,64,512]{2,1,0:T(8,128)(2,1)} %m_hbm.1, s32[1,8]{1,0:T(1,128)} %bitcast.1, bf16[512,512]{1,0:T(8,128)(2,1)} %g_hbm.1, bf16[64,192]{1,0:T(8,128)(2,1)} %gv_hbm.1), custom_call_target="tpu_custom_call" | custom-call | flops 2600000000 | bytes 3145728 | tf_op jit(solution)/shard_map/pallas_call | solution.py:343
  124.1 1.4 %copy.5 = f32[32,16]{0,1:T(8,128)} copy(f32[32,16]{1,0:T(8,128)} %shard_map.46) | data formatting | bytes 4096 | tf_op jit(solution)/shard_map/pallas_call | solution.py:343
